TPU v7x, 32 devices: a whole 2x2x4 slice. The times are simulated.
32 devices in a mesh: dp: 8 (over y, x, core), tensor: 4 (over z).
Axes of the slice: x: 2, y: 2, z: 4, core: 2. Of those that a mesh axis runs over, the one named last changes fastest.
Arguments:
- block_input: bfloat16 [8192, 768], P(('dp', 'tensor')), may hold values from -6 to 6
- doc_lengths: int32 [8, 2], P('dp'), may hold values from 0 to 1024, as said below
- first_gain: bfloat16 [768], P(('dp', 'tensor')), may hold values from 0.5 to 1.5
- first_shift: bfloat16 [768], P(('dp', 'tensor')), may hold values from -1 to 1
- qkv_weight: bfloat16 [768, 3, 768], P('dp', None, 'tensor'), may hold values from -0.21875 to 0.21875
- attn_bias: bfloat16 [1536], P(('dp', 'tensor')), may hold values from -1.5 to 1.5
- out_weight: bfloat16 [768, 768], P('tensor', 'dp'), may hold values from -3.5 to 3.5
- out_bias: bfloat16 [768], P(('dp', 'tensor')), may hold values from -1.5 to 1.5
- second_gain: bfloat16 [768], P(('dp', 'tensor')), may hold values from 0.5 to 1.5
- second_shift: bfloat16 [768], P(('dp', 'tensor')), may hold values from -1 to 1
- fc_weight: bfloat16 [768, 3072], P('dp', 'tensor'), may hold values from -0.21875 to 0.21875
- fc_bias: bfloat16 [3072], P(('dp', 'tensor')), may hold values from -1.5 to 1.5
- proj_weight: bfloat16 [3072, 768], P('tensor', 'dp'), may hold values from -0.109375 to 0.109375
- proj_bias: bfloat16 [768], P(('dp', 'tensor')), may hold values from -1.5 to 1.5
- block_grad: bfloat16 [8192, 768], P(('dp', 'tensor')), may hold values from -6 to 6
Outputs:
- block_out: bfloat16 [8192, 768], P(('dp', 'tensor'))
- input_grad: float32 [8192, 768], P(('dp', 'tensor'))
- first_gain_grad: float32 [768], P(('dp', 'tensor'))
- first_shift_grad: float32 [768], P(('dp', 'tensor'))
- qkv_weight_grad: float32 [768, 3, 768], P('dp', None, 'tensor')
- attn_bias_grad: float32 [1536], P(('dp', 'tensor'))
- out_weight_grad: float32 [768, 768], P('tensor', 'dp')
- out_bias_grad: float32 [768], P(('dp', 'tensor'))
- second_gain_grad: float32 [768], P(('dp', 'tensor'))
- second_shift_grad: float32 [768], P(('dp', 'tensor'))
- fc_weight_grad: float32 [768, 3072], P('dp', 'tensor')
- fc_bias_grad: float32 [3072], P(('dp', 'tensor'))
- proj_weight_grad: float32 [3072, 768], P('tensor', 'dp')
- proj_bias_grad: float32 [768], P(('dp', 'tensor'))
Inputs may be any that keep to these rules, and one draw needn't show every extreme that they name: `doc_lengths`: each row holds the lengths of its group's two documents in order; they sum to 1024, and one of them is longer than 768.
All inputs are finite; a program needn't handle non-finite values.
Results may differ from a plain program's by a relative error of at most 0.019.
Values may be sent and summed in bfloat16 or wider, within the bound.
No kernel may reach another device: no remote copies, remote signals or barrier semaphores. Data moves between devices by JAX's collectives and lax.ppermute only.
A program may use at most 128 MiB of HBM per device.

v0:
```python
import jax
import jax.numpy as jnp
from jax import lax
from jax.sharding import PartitionSpec as P

HEAD_DIM = 64
EPS = 1e-05


def in_blocks(shard, dim, size):
    before, after = (shard.shape[:dim], shard.shape[dim + 1 :])
    return jnp.moveaxis(shard.reshape(*before, size, -1, *after), dim, 0)


def sum_at_owner(shard, axis, dim):
    blocks = in_blocks(shard, dim, lax.axis_size(axis))
    arrived = lax.all_to_all(blocks, axis, split_axis=0, concat_axis=0, tiled=True)
    return arrived.astype(jnp.float32).sum(axis=0)


def norm_rows(values, gain_vec, shift_vec):
    center = jnp.mean(values, axis=-1, keepdims=True)
    offset = values - center
    spread = lax.rsqrt(jnp.mean(offset * offset, axis=-1, keepdims=True) + EPS)
    unit_rows = offset * spread
    return (unit_rows * gain_vec + shift_vec, unit_rows, spread)


def norm_back(grad_out, unit_rows, spread, gain_vec):
    scaled = grad_out * gain_vec
    centred = scaled - jnp.mean(scaled, axis=-1, keepdims=True)
    centred = centred - unit_rows * jnp.mean(scaled * unit_rows, axis=-1, keepdims=True)
    return (spread * centred, jnp.sum(grad_out * unit_rows, axis=0), jnp.sum(grad_out, axis=0))


def gelu_tanh(values):
    return jax.nn.gelu(values, approximate=True)


def fetch_attention(qkv_weight, out_weight):
    return (
        lax.all_gather(qkv_weight, "dp", axis=0, tiled=True),
        lax.all_gather(out_weight, "dp", axis=1, tiled=True),
    )


def gather_ffn(fc_weight, proj_weight):
    return (
        lax.all_gather(fc_weight, "dp", axis=0, tiled=True),
        lax.all_gather(proj_weight, "dp", axis=1, tiled=True),
    )


def scatter_ffn(fc_grad, proj_grad):
    fc_grad, proj_grad = (
        lax.psum_scatter(fc_grad, "dp", scatter_dimension=0, tiled=True),
        lax.psum_scatter(proj_grad, "dp", scatter_dimension=1, tiled=True),
    )
    return (fc_grad, proj_grad)


def rows_forward(values):
    return lax.all_gather(values, "tensor", axis=0, tiled=True)


def sums_forward(values):
    return lax.psum_scatter(
        values.astype(jnp.bfloat16), "tensor", scatter_dimension=0, tiled=True
    ).astype(jnp.float32)


def rows_backward(values):
    return lax.all_gather(values, "tensor", axis=0, tiled=True)


def sums_backward(values):
    return lax.psum_scatter(
        values.astype(jnp.bfloat16), "tensor", scatter_dimension=0, tiled=True
    ).astype(jnp.float32)


def score_block(query_block, key_heads, block_start, boundary, score_scale):
    block_rows = query_block.shape[0]
    key_pos = jnp.arange(key_heads.shape[0])
    query_pos = block_start + jnp.arange(block_rows)
    allowed = (key_pos[None, :] <= query_pos[:, None]) & (
        (key_pos[None, :] >= boundary) == (query_pos[:, None] >= boundary)
    )
    scores = (
        jnp.einsum("ihd,jhd->hij", query_block, key_heads, preferred_element_type=jnp.float32)
        * score_scale
    )
    return jnp.where(allowed[None], scores, -jnp.inf)


def attend(query_heads, key_heads, value_heads, boundary, score_scale):
    row_count, heads_dev, head_dim = query_heads.shape
    block_rows = min(512, row_count)
    outputs = []
    totals = []
    for block_start in range(0, row_count, block_rows):
        scores = score_block(
            query_heads[block_start : block_start + block_rows],
            key_heads,
            block_start,
            boundary,
            score_scale,
        )
        row_peak = jnp.max(scores, axis=-1, keepdims=True)
        log_total = row_peak + jnp.log(jnp.sum(jnp.exp(scores - row_peak), axis=-1, keepdims=True))
        probs_low = jnp.exp(scores - log_total).astype(jnp.bfloat16)
        mixed_block = jnp.einsum(
            "hij,jhd->ihd", probs_low, value_heads, preferred_element_type=jnp.float32
        )
        outputs.append(mixed_block.reshape(block_rows, heads_dev * head_dim).astype(jnp.bfloat16))
        totals.append(log_total)
    return (jnp.concatenate(outputs, axis=0), totals)


def attend_back(query_heads, key_heads, value_heads, totals, grad_heads, boundary, score_scale):
    row_count = query_heads.shape[0]
    block_rows = min(512, row_count)
    query_grads = []
    key_acc = jnp.zeros(key_heads.shape, jnp.float32)
    value_acc = jnp.zeros(value_heads.shape, jnp.float32)
    for block_index, block_start in enumerate(range(0, row_count, block_rows)):
        query_block = query_heads[block_start : block_start + block_rows]
        grad_block = grad_heads[block_start : block_start + block_rows]
        scores = score_block(query_block, key_heads, block_start, boundary, score_scale)
        probs = jnp.exp(scores - totals[block_index])
        probs_low = probs.astype(jnp.bfloat16)
        prob_grads = jnp.einsum(
            "ihd,jhd->hij", grad_block, value_heads, preferred_element_type=jnp.float32
        )
        row_dot = jnp.sum(probs * prob_grads, axis=-1, keepdims=True)
        score_grads = (probs * (prob_grads - row_dot)).astype(jnp.bfloat16)
        query_grads.append(
            jnp.einsum("hij,jhd->ihd", score_grads, key_heads, preferred_element_type=jnp.float32)
            * score_scale
        )
        key_acc = key_acc + jnp.einsum(
            "hij,ihd->jhd", score_grads, query_block, preferred_element_type=jnp.float32
        )
        value_acc = value_acc + jnp.einsum(
            "hij,ihd->jhd", probs_low, grad_block, preferred_element_type=jnp.float32
        )
    return (jnp.concatenate(query_grads, axis=0), key_acc * score_scale, value_acc)


def body(
    block_input,
    doc_lengths,
    first_gain,
    first_shift,
    qkv_weight,
    attn_bias,
    out_weight,
    out_bias,
    second_gain,
    second_shift,
    fc_weight,
    fc_bias,
    proj_weight,
    proj_bias,
    block_grad,
):
    small_params = (
        lax.all_gather(first_gain, ("dp", "tensor"), axis=0, tiled=True),
        lax.all_gather(first_shift, ("dp", "tensor"), axis=0, tiled=True),
        lax.all_gather(attn_bias, ("dp", "tensor"), axis=0, tiled=True),
        lax.all_gather(out_bias, ("dp", "tensor"), axis=0, tiled=True),
        lax.all_gather(second_gain, ("dp", "tensor"), axis=0, tiled=True),
        lax.all_gather(second_shift, ("dp", "tensor"), axis=0, tiled=True),
        lax.all_gather(fc_bias, ("dp", "tensor"), axis=0, tiled=True),
        lax.all_gather(proj_bias, ("dp", "tensor"), axis=0, tiled=True),
    )
    gain_one, shift_one, attn_shift, out_shift, gain_two, shift_two, fc_shift, proj_shift = tuple(
        (param.astype(jnp.float32) for param in small_params)
    )
    tensor_rank = lax.axis_index("tensor")
    width = block_input.shape[1]
    width_dev = qkv_weight.shape[2]
    head_dim = HEAD_DIM
    heads_dev = width_dev // head_dim
    score_scale = head_dim ** (-0.5)
    boundary = doc_lengths[0, 0]
    qkv_full, out_full = fetch_attention(qkv_weight, out_weight)
    inputs = block_input.astype(jnp.float32)
    normed_one, unit_one, spread_one = norm_rows(inputs, gain_one, shift_one)
    rows_one = rows_forward(normed_one.astype(jnp.bfloat16))
    row_count = rows_one.shape[0]
    projected = jnp.einsum("ic,cpd->ipd", rows_one, qkv_full, preferred_element_type=jnp.float32)
    query_shift = lax.dynamic_slice_in_dim(attn_shift, tensor_rank * width_dev, width_dev)
    value_shift = lax.dynamic_slice_in_dim(attn_shift, width + tensor_rank * width_dev, width_dev)
    head_shape = (row_count, heads_dev, head_dim)
    queries = (projected[:, 0] + query_shift).astype(jnp.bfloat16).reshape(head_shape)
    key_rows = projected[:, 1].astype(jnp.bfloat16).reshape(head_shape)
    value_rows = (projected[:, 2] + value_shift).astype(jnp.bfloat16).reshape(head_shape)
    mixed_heads, totals = attend(queries, key_rows, value_rows, boundary, score_scale)
    attn_part = jnp.dot(mixed_heads, out_full, preferred_element_type=jnp.float32)
    hidden = inputs + (sums_forward(attn_part) + out_shift)
    normed_two, unit_two, spread_two = norm_rows(hidden, gain_two, shift_two)
    normed_two = normed_two.astype(jnp.bfloat16)
    fc_full, proj_full = gather_ffn(fc_weight, proj_weight)
    hidden_dev = fc_full.shape[1]
    rows_two = rows_forward(normed_two)
    fc_slice = lax.dynamic_slice_in_dim(fc_shift, tensor_rank * hidden_dev, hidden_dev)
    pre_act = jnp.dot(rows_two, fc_full, preferred_element_type=jnp.float32) + fc_slice
    gelu_values, gelu_pull = jax.vjp(gelu_tanh, pre_act)
    activated = gelu_values.astype(jnp.bfloat16)
    mlp_part = jnp.dot(activated, proj_full, preferred_element_type=jnp.float32)
    mlp_out = sums_forward(mlp_part) + proj_shift
    block_out = (hidden + mlp_out).astype(jnp.bfloat16)
    top_grad = block_grad.astype(jnp.float32)
    proj_bias_grad = jnp.sum(top_grad, axis=0)
    fc_back, proj_back = gather_ffn(fc_weight, proj_weight)
    rows_grad = rows_backward(block_grad)
    proj_grad = jnp.einsum("if,id->fd", activated, rows_grad, preferred_element_type=jnp.float32)
    act_grad = jnp.einsum("id,fd->if", rows_grad, proj_back, preferred_element_type=jnp.float32)
    pre_grad = gelu_pull(act_grad)[0].astype(jnp.bfloat16)
    fc_grad = jnp.einsum("ic,if->cf", rows_two, pre_grad, preferred_element_type=jnp.float32)
    fc_cols = jnp.sum(pre_grad.astype(jnp.float32), axis=0)
    normed_two_grad = jnp.einsum("if,cf->ic", pre_grad, fc_back, preferred_element_type=jnp.float32)
    normed_two_grad = sums_backward(normed_two_grad)
    fc_bias_grad = lax.dynamic_update_slice_in_dim(
        jnp.zeros((fc_shift.shape[0],), jnp.float32), fc_cols, tensor_rank * hidden_dev, 0
    )
    fc_weight_grad, proj_weight_grad = scatter_ffn(fc_grad, proj_grad)
    hidden_part, second_gain_grad, second_shift_grad = norm_back(
        normed_two_grad, unit_two, spread_two, gain_two
    )
    hidden_grad = top_grad + hidden_part
    attn_grad = hidden_grad.astype(jnp.bfloat16)
    out_bias_grad = jnp.sum(attn_grad.astype(jnp.float32), axis=0)
    rows_attn = rows_backward(attn_grad)
    qkv_back, out_back = fetch_attention(qkv_weight, out_weight)
    out_grad = jnp.einsum("ik,id->kd", mixed_heads, rows_attn, preferred_element_type=jnp.float32)
    heads_grad = jnp.einsum(
        "id,kd->ik", rows_attn, out_back, preferred_element_type=jnp.float32
    ).astype(jnp.bfloat16)
    query_grad, key_grad, value_grad = attend_back(
        queries, key_rows, value_rows, totals, heads_grad.reshape(head_shape), boundary, score_scale
    )
    flat_shape = (row_count, width_dev)
    query_low = query_grad.reshape(flat_shape).astype(jnp.bfloat16)
    value_low = value_grad.reshape(flat_shape).astype(jnp.bfloat16)
    projection_grads = jnp.stack(
        [query_low, key_grad.reshape(flat_shape).astype(jnp.bfloat16), value_low], axis=1
    )
    qkv_grad = jnp.einsum(
        "ic,ipd->cpd", rows_one, projection_grads, preferred_element_type=jnp.float32
    )
    normed_one_grad = jnp.einsum(
        "ipd,cpd->ic", projection_grads, qkv_back, preferred_element_type=jnp.float32
    )
    normed_one_grad = sums_backward(normed_one_grad)
    attn_bias_grad = jnp.zeros((2 * width,), jnp.float32)
    attn_bias_grad = lax.dynamic_update_slice_in_dim(
        attn_bias_grad, jnp.sum(query_low.astype(jnp.float32), axis=0), tensor_rank * width_dev, 0
    )
    attn_bias_grad = lax.dynamic_update_slice_in_dim(
        attn_bias_grad,
        jnp.sum(value_low.astype(jnp.float32), axis=0),
        width + tensor_rank * width_dev,
        0,
    )
    qkv_weight_grad, out_weight_grad = (
        sum_at_owner(qkv_grad.astype(jnp.bfloat16), "dp", 0),
        sum_at_owner(out_grad.astype(jnp.bfloat16), "dp", 1),
    )
    input_part, first_gain_grad, first_shift_grad = norm_back(
        normed_one_grad, unit_one, spread_one, gain_one
    )
    input_grad = hidden_grad + input_part
    (
        first_gain_grad,
        first_shift_grad,
        attn_bias_grad,
        out_bias_grad,
        second_gain_grad,
        second_shift_grad,
        fc_bias_grad,
        proj_bias_grad,
    ) = (
        lax.psum_scatter(first_gain_grad, ("dp", "tensor"), scatter_dimension=0, tiled=True),
        lax.psum_scatter(first_shift_grad, ("dp", "tensor"), scatter_dimension=0, tiled=True),
        lax.psum_scatter(attn_bias_grad, ("dp", "tensor"), scatter_dimension=0, tiled=True),
        lax.psum_scatter(out_bias_grad, ("dp", "tensor"), scatter_dimension=0, tiled=True),
        lax.psum_scatter(second_gain_grad, ("dp", "tensor"), scatter_dimension=0, tiled=True),
        lax.psum_scatter(second_shift_grad, ("dp", "tensor"), scatter_dimension=0, tiled=True),
        lax.psum_scatter(fc_bias_grad, ("dp", "tensor"), scatter_dimension=0, tiled=True),
        lax.psum_scatter(proj_bias_grad, ("dp", "tensor"), scatter_dimension=0, tiled=True),
    )
    return (
        block_out,
        input_grad,
        first_gain_grad,
        first_shift_grad,
        qkv_weight_grad,
        attn_bias_grad,
        out_weight_grad,
        out_bias_grad,
        second_gain_grad,
        second_shift_grad,
        fc_weight_grad,
        fc_bias_grad,
        proj_weight_grad,
        proj_bias_grad,
    )


def solution(mesh):
    return jax.shard_map(
        body,
        mesh=mesh,
        in_specs=(
            P(("dp", "tensor"), None),
            P("dp", None),
            P(("dp", "tensor")),
            P(("dp", "tensor")),
            P("dp", None, "tensor"),
            P(("dp", "tensor")),
            P("tensor", "dp"),
            P(("dp", "tensor")),
            P(("dp", "tensor")),
            P(("dp", "tensor")),
            P("dp", "tensor"),
            P(("dp", "tensor")),
            P("tensor", "dp"),
            P(("dp", "tensor")),
            P(("dp", "tensor"), None),
        ),
        out_specs=(
            P(("dp", "tensor"), None),
            P(("dp", "tensor"), None),
            P(("dp", "tensor")),
            P(("dp", "tensor")),
            P("dp", None, "tensor"),
            P(("dp", "tensor")),
            P("tensor", "dp"),
            P(("dp", "tensor")),
            P(("dp", "tensor")),
            P(("dp", "tensor")),
            P("dp", "tensor"),
            P(("dp", "tensor")),
            P("tensor", "dp"),
            P(("dp", "tensor")),
        ),
        check_vma=False,
    )
```

profile of v0, /device:TPU:0, one launch (start us, length us, event | category | flops | bytes accessed | tf_op | source)
XLA Modules:
  0.0 531.3 jit_solution(13650693505043165008)
XLA Ops:
  17.2 42.4 %all-reduce.17 = (bf16[1536]{0:T(1024)(128)(2,1)S(1)}, bf16[768]{0:T(1024)(128)(2,1)S(1)}, bf16[768]{0:T(1024)(128)(2,1)S(1)}, bf16[768]{0:T(1024)(128)(2,1)S(1)...) all-reduce(bf16[1536]{0:T(1024)(128)(2,1)S(1)} %dynamic-update-slic, ...), channel_id=1, replica_groups=mesh['dp'=8,'tensor'=4] {'dp','tensor'}, use_global_device_ids=true, to_apply=%add.2 | all-reduce | flops 9216 | bytes 36864
  59.6 2.0 fusion.29
  63.8 12.9 %all_gather.55 = bf16[768,3,192]{2,1,0:T(4,128)(2,1)S(1)} all-gather(bf16[96,3,192]{2,1,0:T(4,128)(2,1)S(1)} %copy.31), channel_id=1, replica_groups=mesh['dp'=8,'tensor'=4] {'dp'}, dimensions={0}, use_global_device_ids=true | all-gather | bytes 995328 | tf_op jit(solution)/shard_map/all_gather | solution.py:42
  77.5 10.3 %all_gather.57 = bf16[192,768]{0,1:T(8,128)(2,1)S(1)} all-gather(bf16[192,96]{0,1:T(8,128)(2,1)S(1)} %copy.33), channel_id=1, replica_groups=mesh['dp'=8,'tensor'=4] {'dp'}, dimensions={1}, use_global_device_ids=true | all-gather | bytes 331776 | tf_op jit(solution)/shard_map/all_gather | solution.py:43
  89.1 9.6 %all-gather.7.cloned.1.call-done = bf16[1024,768]{1,0:T(8,128)(2,1)} async-done(((bf16[256,768]{1,0:T(8,128)(2,1)}), bf16[1024,768]{1,0:T(8,128)(2,1)}) %all-gather.7.cloned.1.call-update) | async-done | bytes 1572880 | tf_op jit(solution)/shard_map/all_gather | solution.py:63
  98.7 2.5 fusion.55
  101.5 1.3 fusion
  102.9 1.7 exponential_reduce_fusion.1
  104.6 1.3 fusion.1
  106.0 1.7 exponential_reduce_fusion
  107.8 1.9 convolution_convert_fusion.6
  109.7 1.9 convolution_convert_fusion.5
  112.3 1.8 convolution_convert_fusion.2
  114.8 33.6 %reduce-scatter.7.cloned.1.call-done = bf16[256,768]{1,0:T(8,128)(2,1)} async-done(((bf16[1024,768]{1,0:T(8,128)(2,1)}), bf16[256,768]{1,0:T(8,128)(2,1)}) %reduce-scatter.7.cloned.1.call-update) | async-done | bytes 393232 | tf_op jit(solution)/shard_map/reduce_scatter | solution.py:67
  150.9 2.0 add_convert_fusion.1
  154.6 34.4 %all-gather.9.cloned.1.call-done = bf16[1024,768]{1,0:T(8,128)(2,1)} async-done(((bf16[256,768]{1,0:T(8,128)(2,1)}), bf16[1024,768]{1,0:T(8,128)(2,1)}) %all-gather.9.cloned.1.call-update) | async-done | bytes 1572880 | tf_op jit(solution)/shard_map/all_gather | solution.py:63
  189.0 4.8 fusion.56
  193.8 19.7 %all-gather.13.cloned.1.call-done = bf16[768,768]{0,1:T(8,128)(2,1)} async-done(((bf16[768,96]{0,1:T(8,128)(2,1)}), bf16[768,768]{0,1:T(8,128)(2,1)}) %all-gather.13.cloned.1.call-update) | async-done | bytes 1179664 | tf_op jit(solution)/shard_map/all_gather | solution.py:50
  213.5 38.5 %all-gather.15.cloned.1.call-done = bf16[1024,768]{1,0:T(8,128)(2,1)} async-done(((bf16[256,768]{1,0:T(8,128)(2,1)}), bf16[1024,768]{1,0:T(8,128)(2,1)}) %all-gather.15.cloned.1.call-update) | async-done | bytes 1572880 | tf_op jit(solution)/shard_map/all_gather | solution.py:73
  252.0 6.4 %convert_reduce_fusion = (f32[768]{0:T(1024)}, bf16[1024,768]{1,0:T(8,128)(2,1)S(1)}) fusion(f32[1024,768]{1,0:T(8,128)} %fusion.56, f32[768]{0:T(1024)S(1)} %dynamic-slice_convert_fusion, bf16[1024,768]{1,0:T(8,128)(2,1)} %all-gather.15.cloned.1.call-done, bf16[768,768]{0,1:T(8,128)(2,1)} %all-gather.13.cloned.1.call-done), kind=kOutput, calls=%fused_computation.24 | convolution fusion | flops 1226046720 | bytes 7477248 | tf_op jit(solution)/shard_map/id,fd->if/dot_general | solution.py:219
  259.6 2.6 convolution_convert_fusion
  262.3 5.6 %convolution_convert_fusion.1 = bf16[1024,768]{1,0:T(8,128)(2,1)} fusion(bf16[768,768]{0,1:T(8,128)(2,1)} %all-gather.13.cloned.1.call-done, f32[1024,768]{1,0:T(8,128)} %fusion.56, f32[768]{0:T(1024)S(1)} %dynamic-slice_convert_fusion), kind=kOutput, calls=%fused_computation.32 | convolution fusion | flops 1216610304 | bytes 5901312 | tf_op jit(solution)/shard_map/dot_general | solution.py:211
  267.9 28.6 %reduce-scatter.11.cloned.1.call-done = bf16[256,768]{1,0:T(8,128)(2,1)} async-done(((bf16[1024,768]{1,0:T(8,128)(2,1)}), bf16[256,768]{1,0:T(8,128)(2,1)}) %reduce-scatter.11.cloned.1.call-update) | async-done | bytes 393232 | tf_op jit(solution)/shard_map/reduce_scatter | solution.py:77
  296.5 2.1 fusion.38
  298.6 34.3 %reduce-scatter.9.cloned.1.call-done = bf16[256,768]{1,0:T(8,128)(2,1)} async-done(((bf16[1024,768]{1,0:T(8,128)(2,1)}), bf16[256,768]{1,0:T(8,128)(2,1)}) %reduce-scatter.9.cloned.1.call-update) | async-done | bytes 393232 | tf_op jit(solution)/shard_map/reduce_scatter | solution.py:67
  332.9 3.5 convert_reduce_fusion.6
  336.5 36.0 %all-gather.17.cloned.1.call-done = bf16[1024,768]{1,0:T(8,128)(2,1)} async-done(((bf16[256,768]{1,0:T(8,128)(2,1)}), bf16[1024,768]{1,0:T(8,128)(2,1)}) %all-gather.17.cloned.1.call-update) | async-done | bytes 1572880 | tf_op jit(solution)/shard_map/all_gather | solution.py:73
  372.5 2.2 convolution_convert_fusion.3
  374.8 4.7 fusion.47
  379.5 2.5 multiply_reduce_fusion.1
  382.0 2.0 multiply_convert_fusion.1
  385.9 2.5 multiply_reduce_fusion
  388.4 2.6 convert_reduce_fusion.8
  391.0 1.8 multiply_convert_fusion
  395.1 2.6 bitcast_convert_fusion
  397.8 5.1 fusion.50
  403.3 4.9 fusion.58
  408.2 1.5 convolution_convert_fusion.4
  411.0 3.7 all-to-all-start.1
  414.8 2.5 fusion.59
  418.6 1.3 copy.35
  420.0 3.0 all-to-all-done.1
  423.0 3.6 all-to-all-start
  428.2 15.1 %all-to-all-done = bf16[8,96,3,192]{1,3,2,0:T(8,128)(2,1)S(1)} async-done(((bf16[8,96,3,192]{1,3,2,0:T(8,128)(2,1)}), bf16[8,96,3,192]{1,3,2,0:T(8,128)(2,1)S(1)}, u32[]{:S(2)}, u32[]{:S(2)}) %all-to-all-start) | async-done | bytes 884768 | tf_op jit(solution)/shard_map/all_to_all | solution.py:17
  444.4 1.5 fusion.39
  445.9 39.5 %all-reduce.16 = (f32[768]{0:T(1024)S(1)}, f32[768]{0:T(1024)S(1)}, f32[1536]{0:T(1024)S(1)}, f32[768]{0:T(1024)S(1)}, f32[768]{0:T(1024)S(1)}, /*index=5*/f32[7...) all-reduce(f32[768]{0:T(1024)S(1)} %get-tuple-element.30, ...), channel_id=6, replica_groups=mesh['dp'=8,'tensor'=4] {'dp','tensor'}, use_global_device_ids=true, to_apply=%region_19.20.clone | all-reduce | flops 9216 | bytes 73728
  490.1 2.2 fusion.32
  492.3 31.4 %reduce-scatter.15.cloned.1.call-done = f32[96,768]{1,0:T(8,128)} async-done(((f32[768,768]{1,0:T(8,128)}), f32[96,768]{1,0:T(8,128)}) %reduce-scatter.15.cloned.1.call-update) | async-done | bytes 294928 | tf_op jit(solution)/shard_map/reduce_scatter | solution.py:56
  (165 shorter events, 35.2 us)
Async XLA Ops:
  8.0 90.7 %all-gather.7.cloned.1.call-start = ((), (), s32[]{:S(2)}) async-start(), calls=%async_computation.8 | async-start | bytes 1966080 | tf_op jit(solution)/shard_map/all_gather | solution.py:63
  10.5 51.4 %copy-start.10 = (f32[256]{0:T(256)}, f32[256]{0:T(256)S(1)}, u32[]{:S(2)}) copy-start(f32[256]{0:T(256)S(1)} %add_rsqrt_fusion.1) | copy-start | bytes 3076
  59.6 28.2 %copy-start.22 = (s32[1,2]{1,0:T(1,128)S(1)}, s32[1,2]{1,0:T(1,128)}, u32[]{:S(2)}) copy-start(s32[1,2]{1,0:T(1,128)} %param.16) | copy-start | bytes 28
  61.6 86.8 %reduce-scatter.7.cloned.1.call-start = ((), (), s32[]{:S(2)}) async-start(), calls=%async_computation.9 | async-start | bytes 1966080 | tf_op jit(solution)/shard_map/reduce_scatter | solution.py:67
  77.5 23.7 %copy-start.6 = (bf16[768,3,192]{0,2,1:T(8,128)(2,1)}, bf16[768,3,192]{0,2,1:T(8,128)(2,1)S(1)}, u32[]{:S(2)}) copy-start(bf16[768,3,192]{0,2,1:T(8,128)(2,1)S(1)} %copy.32) | copy-start | bytes 2654212
  102.9 5.0 copy-start.1
  106.0 3.8 copy-start
  109.7 1.9 copy-start.8
  111.6 0.7 copy-start.9
  111.6 36.8 %copy-start.2 = (bf16[256,768]{1,0:T(8,128)(2,1)S(1)}, bf16[256,768]{1,0:T(8,128)(2,1)}, u32[]{:S(2)}) copy-start(bf16[256,768]{1,0:T(8,128)(2,1)} %param.15) | copy-start | bytes 1179652
  114.2 40.4 %all-gather.11.cloned.1.call-start = ((), (), s32[]{:S(2)}) async-start(), calls=%async_computation.11 | async-start | bytes 1327104 | tf_op jit(solution)/shard_map/all_gather | solution.py:49
  114.7 74.2 %all-gather.9.cloned.1.call-start = ((), (), s32[]{:S(2)}) async-start(), calls=%async_computation.10 | async-start | bytes 1966080 | tf_op jit(solution)/shard_map/all_gather | solution.py:63
  152.9 60.5 %all-gather.13.cloned.1.call-start = ((), (), s32[]{:S(2)}) async-start(), calls=%async_computation.12 | async-start | bytes 1327104 | tf_op jit(solution)/shard_map/all_gather | solution.py:50
  153.5 98.5 %all-gather.15.cloned.1.call-start = ((), (), s32[]{:S(2)}) async-start(), calls=%async_computation.14 | async-start | bytes 1966080 | tf_op jit(solution)/shard_map/all_gather | solution.py:73
  154.3 142.2 %reduce-scatter.11.cloned.1.call-start = ((), (), s32[]{:S(2)}) async-start(), calls=%async_computation.15 | async-start | bytes 1966080 | tf_op jit(solution)/shard_map/reduce_scatter | solution.py:77
  154.6 107.7 %copy-start.17 = (f32[768]{0:T(1024)}, f32[768]{0:T(1024)S(1)}, u32[]{:S(2)}) copy-start(f32[768]{0:T(1024)S(1)} %dynamic-slice_convert_fusion) | copy-start | bytes 9220
  252.0 7.6 %copy-start.21 = (bf16[768,768]{1,0:T(8,128)(2,1)S(1)}, bf16[768,768]{1,0:T(8,128)(2,1)}, u32[]{:S(2)}) copy-start(bf16[768,768]{1,0:T(8,128)(2,1)} %all-gather.11.cloned.1.call-done) | copy-start | bytes 3538948
  258.4 1.2 copy-start.23
  262.2 34.3 %copy-start.3 = (bf16[256,768]{1,0:T(8,128)(2,1)S(1)}, bf16[256,768]{1,0:T(8,128)(2,1)}, u32[]{:S(2)}) copy-start(bf16[256,768]{1,0:T(8,128)(2,1)} %reduce-scatter.7.cloned.1.call-done) | copy-start | bytes 1179652
  262.2 70.7 %reduce-scatter.9.cloned.1.call-start = ((), (), s32[]{:S(2)}) async-start(), calls=%async_computation.13 | async-start | bytes 1966080 | tf_op jit(solution)/shard_map/reduce_scatter | solution.py:67
  267.9 104.7 %all-gather.17.cloned.1.call-start = ((), (), s32[]{:S(2)}) async-start(), calls=%async_computation.16 | async-start | bytes 1966080 | tf_op jit(solution)/shard_map/all_gather | solution.py:73
  336.5 107.9 %reduce-scatter.13.cloned.1.call-start = ((), (), s32[]{:S(2)}) async-start(), calls=%async_computation.17 | async-start | bytes 1966080 | tf_op jit(solution)/shard_map/reduce_scatter | solution.py:77
  372.5 7.0 %slice-start.2 = ((s8[6291456]{0:T(1024)(128)(4,1)}), s8[4194304]{0:T(1024)(128)(4,1)S(1)}, s32[]{:S(2)}) async-start(s8[6291456]{0:T(1024)(128)(4,1)} %bitcast.83), calls=%async_computation.22 | async-start | bytes 8388608
  374.8 4.7 slice-start.3
  379.5 6.3 %slice-start = ((s8[6291456]{0:T(1024)(128)(4,1)}), s8[4194304]{0:T(1024)(128)(4,1)S(1)}, s32[]{:S(2)}) async-start(s8[6291456]{0:T(1024)(128)(4,1)} %bitcast.81), calls=%async_computation.20 | async-start | bytes 8388608
  382.0 3.9 slice-start.1
  393.9 1.2 copy-start.7
  395.1 2.7 copy-start.18
  395.1 2.7 copy-start.20
  397.7 94.6 %reduce-scatter.17.cloned.1.call-start = ((), (), s32[]{:S(2)}) async-start(), calls=%async_computation.19 | async-start | bytes 2654208 | tf_op jit(solution)/shard_map/reduce_scatter | solution.py:57
  403.0 5.2 copy-start.5
  403.0 120.7 %reduce-scatter.15.cloned.1.call-start = ((), (), s32[]{:S(2)}) async-start(), calls=%async_computation.18 | async-start | bytes 2654208 | tf_op jit(solution)/shard_map/reduce_scatter | solution.py:56
  411.0 12.0 %all-to-all-start.1 = ((bf16[8,192,96]{2,1,0:T(8,128)(2,1)}), bf16[8,192,96]{2,1,0:T(8,128)(2,1)S(1)}, u32[]{:S(2)}, u32[]{:S(2)}) async-start(bf16[8,192,96]{2,1,0:T(8,128)(2,1)} %bitcast.79), calls=%async_computation.5 | async-start | bytes 786432 | tf_op jit(solution)/shard_map/all_to_all | solution.py:17
  417.4 9.2 %copy-start.16 = (f32[768]{0:T(1024)S(1)}, f32[768]{0:T(1024)}, u32[]{:S(2)}) copy-start(f32[768]{0:T(1024)} %get-tuple-element.52) | copy-start | bytes 9220
  417.4 9.5 %copy-start.19 = (f32[3,64]{1,0:T(4,128)S(1)}, f32[3,64]{1,0:T(4,128)}, u32[]{:S(2)}) copy-start(f32[3,64]{1,0:T(4,128)} %get-tuple-element.77) | copy-start | bytes 2308
  418.6 25.8 %copy-start.11 = (f32[256]{0:T(256)S(1)}, f32[256]{0:T(256)}, u32[]{:S(2)}) copy-start(f32[256]{0:T(256)} %copy-done.10) | copy-start | bytes 3076
  419.9 26.0 %copy-start.12 = (f32[768]{0:T(1024)S(1)}, f32[768]{0:T(1024)}, u32[]{:S(2)}) copy-start(f32[768]{0:T(1024)} %get-tuple-element.28) | copy-start | bytes 9220
  419.9 26.0 %copy-start.13 = (f32[768]{0:T(1024)S(1)}, f32[768]{0:T(1024)}, u32[]{:S(2)}) copy-start(f32[768]{0:T(1024)} %get-tuple-element.34) | copy-start | bytes 9220
  419.9 26.0 %copy-start.14 = (f32[768]{0:T(1024)S(1)}, f32[768]{0:T(1024)}, u32[]{:S(2)}) copy-start(f32[768]{0:T(1024)} %get-tuple-element.54) | copy-start | bytes 9220
  419.9 26.0 %copy-start.15 = (f32[768]{0:T(1024)S(1)}, f32[768]{0:T(1024)}, u32[]{:S(2)}) copy-start(f32[768]{0:T(1024)} %get-tuple-element.60) | copy-start | bytes 9220
  419.9 70.2 %copy-start.4 = (f32[256,768]{1,0:T(8,128)S(1)}, f32[256,768]{1,0:T(8,128)}, u32[]{:S(2)}) copy-start(f32[256,768]{1,0:T(8,128)} %get-tuple-element.56) | copy-start | bytes 2359300
  423.0 20.3 %all-to-all-start = ((bf16[8,96,3,192]{1,3,2,0:T(8,128)(2,1)}), bf16[8,96,3,192]{1,3,2,0:T(8,128)(2,1)S(1)}, u32[]{:S(2)}, u32[]{:S(2)}) async-start(bf16[8,96,3,192]{1,3,2,0:T(8,128)(2,1)} %copy.35), calls=%async_computation.4 | async-start | bytes 2359296 | tf_op jit(solution)/shard_map/all_to_all | solution.py:17
Sparse Core Ops, SparseCore 0:
  61.7 36.9 all-gather.6
  114.3 34.1 reduce-scatter.6
  262.3 34.1 reduce-scatter.10
  298.7 34.2 reduce-scatter.8
Sparse Core Ops, SparseCore 1:
  116.5 22.7 all-gather.10
  153.0 35.9 all-gather.8
  190.7 22.7 all-gather.12
  215.1 36.9 all-gather.14
  336.6 35.9 all-gather.16
  397.8 34.1 reduce-scatter.12
  435.8 41.3 reduce-scatter.16
  481.3 42.4 reduce-scatter.14
where the time goes:
time: 536 us; the launch traced here: 531 us
  waiting for transfers between devices  286 us (53%)
  blocking collectives  105 us (20%)
  matrix products  64.9 us (12%)
  other arithmetic  28.4 us (5%)
  local copies, waits for them, and re-layouts  22.3 us (4%)
  between operations  16.4 us (3%)
  starting transfers between devices  8.17 us (2%)
    unnamed x2, blocking collectives  81.9 us
    all_gather x2, waiting for transfers between devices, rows_backward(): return lax.all_gather(values, 'tensor', axis=0, tiled=True)  74.5 us
    reduce_scatter x2, waiting for transfers between devices, sums_forward(): lax.psum_scatter(values.astype(jnp.bfloat16), 'tensor', scatter_dimension...  68 us
    all_gather x2, waiting for transfers between devices, rows_forward(): return lax.all_gather(values, 'tensor', axis=0, tiled=True)  44 us
    reduce_scatter x1, waiting for transfers between devices, scatter_ffn(): lax.psum_scatter(fc_grad, 'dp', scatter_dimension=0, tiled=True)  31.4 us
    reduce_scatter x2, waiting for transfers between devices, sums_backward(): lax.psum_scatter(values.astype(jnp.bfloat16), 'tensor', scatter_dimension...  28.6 us
    all_gather x1, waiting for transfers between devices, gather_ffn(): lax.all_gather(proj_weight, 'dp', axis=1, tiled=True)  19.7 us
    all_to_all x2, waiting for transfers between devices, sum_at_owner(): lax.all_to_all(blocks, axis, split_axis=0, concat_axis=0, tiled=True)  18.1 us
  transfers between devices with their start and end apart: 14, of which 11 were waited for; matrix products, arithmetic and copies ran while one was open for 9% of the time, Pallas kernels for 0%

commit v1 on v0

--- a/solution.py
+++ b/solution.py
@@ -5,6 +5,18 @@
 
 HEAD_DIM = 64
 EPS = 1e-05
+
+
+def gather_by_bits(value, axis, dim):
+    ways, here, lap = (lax.axis_size(axis), lax.axis_index(axis), value.shape[dim])
+    line, have = (value, 1)
+    while have < ways:
+        line = jnp.concatenate(
+            [line, lax.ppermute(line, axis, [(d, (d - have) % ways) for d in range(ways)])],
+            axis=dim,
+        )
+        have = 2 * have
+    return jnp.roll(line, here * lap, axis=dim)
 
 
 def in_blocks(shard, dim, size):
@@ -47,7 +59,7 @@
 def gather_ffn(fc_weight, proj_weight):
     return (
         lax.all_gather(fc_weight, "dp", axis=0, tiled=True),
-        lax.all_gather(proj_weight, "dp", axis=1, tiled=True),
+        gather_by_bits(proj_weight, "dp", 1),
     )
 
 

time: 536 us -> 510 us (0.951)
  waiting for transfers between devices: 286 us -> 249 us
  other arithmetic: 28.4 us -> 35.9 us
    all_gather x2, waiting for transfers between devices: 44 us -> 9.6 us  [rows_forward(): return lax.all_gather(values, 'tensor', axis=0, tiled=True)]
    ppermute x0 -> x3, waiting for transfers between devices: none -> 26.2 us  [gather_by_bits(): lax.ppermute(line, axis, [(d, (d - have) % ways) for d in range(ways)])]
    all_gather x1 -> x0, waiting for transfers between devices: 19.7 us -> none  [gather_ffn(): lax.all_gather(proj_weight, 'dp', axis=1, tiled=True)]
    all_gather x2, waiting for transfers between devices: 74.5 us -> 66.3 us  [rows_backward(): return lax.all_gather(values, 'tensor', axis=0, tiled=True)]
    concatenate x0 -> x3, other arithmetic: none -> 7.29 us  [the longest x1 6.42 us: gather_by_bits(): return jnp.roll(line, here * lap, axis=dim)]
    unnamed x83 -> x87, local copies, waits for them, and re-layouts: 16.4 us -> 17.2 us
  transfers between devices with their start and end apart: 14 -> 16, of which waited for: 11 -> 12; matrix products, arithmetic and copies ran while one was open for 9% -> 11% of each run, Pallas kernels for 0% -> 0%
where the time goes in v1:
time: 510 us; the launch traced here: 505 us
  waiting for transfers between devices  249 us (49%)
  blocking collectives  105 us (21%)
  matrix products  64.8 us (13%)
  other arithmetic  35.9 us (7%)
  local copies, waits for them, and re-layouts  23 us (5%)
  between operations  16.1 us (3%)
  starting transfers between devices  11.1 us (2%)
    unnamed x2, blocking collectives  81.9 us
    reduce_scatter x2, waiting for transfers between devices, sums_forward(): lax.psum_scatter(values.astype(jnp.bfloat16), 'tensor', scatter_dimension...  68 us
    all_gather x2, waiting for transfers between devices, rows_backward(): return lax.all_gather(values, 'tensor', axis=0, tiled=True)  66.3 us
    reduce_scatter x1, waiting for transfers between devices, scatter_ffn(): lax.psum_scatter(fc_grad, 'dp', scatter_dimension=0, tiled=True)  31.6 us
    reduce_scatter x2, waiting for transfers between devices, sums_backward(): lax.psum_scatter(values.astype(jnp.bfloat16), 'tensor', scatter_dimension...  28.6 us
    ppermute x3, waiting for transfers between devices, gather_by_bits(): lax.ppermute(line, axis, [(d, (d - have) % ways) for d in range(ways)])  26.2 us
    all_to_all x2, waiting for transfers between devices, sum_at_owner(): lax.all_to_all(blocks, axis, split_axis=0, concat_axis=0, tiled=True)  18.1 us
    unnamed x87, local copies, waits for them, and re-layouts  17.2 us
  transfers between devices with their start and end apart: 16, of which 12 were waited for; matrix products, arithmetic and copies ran while one was open for 11% of the time, Pallas kernels for 0%

profile of v1, /device:TPU:0, one launch (start us, length us, event | category | flops | bytes accessed | tf_op | source)
XLA Modules:
  0.0 505.5 jit_solution(907564977487804330)
XLA Ops:
  17.2 42.4 %all-reduce.17 = (bf16[1536]{0:T(1024)(128)(2,1)S(1)}, bf16[768]{0:T(1024)(128)(2,1)S(1)}, bf16[768]{0:T(1024)(128)(2,1)S(1)}, bf16[768]{0:T(1024)(128)(2,1)S(1)...) all-reduce(bf16[1536]{0:T(1024)(128)(2,1)S(1)} %dynamic-update-slic, ...), channel_id=1, replica_groups=mesh['dp'=8,'tensor'=4] {'dp','tensor'}, use_global_device_ids=true, to_apply=%add.2 | all-reduce | flops 9216 | bytes 36864
  59.6 2.0 fusion.39
  63.8 12.9 %all_gather.51 = bf16[768,3,192]{2,1,0:T(4,128)(2,1)S(1)} all-gather(bf16[96,3,192]{2,1,0:T(4,128)(2,1)S(1)} %copy.32), channel_id=1, replica_groups=mesh['dp'=8,'tensor'=4] {'dp'}, dimensions={0}, use_global_device_ids=true | all-gather | bytes 995328 | tf_op jit(solution)/shard_map/all_gather | solution.py:54
  77.5 10.3 %all_gather.53 = bf16[192,768]{0,1:T(8,128)(2,1)S(1)} all-gather(bf16[192,96]{0,1:T(8,128)(2,1)S(1)} %copy.34), channel_id=1, replica_groups=mesh['dp'=8,'tensor'=4] {'dp'}, dimensions={1}, use_global_device_ids=true | all-gather | bytes 331776 | tf_op jit(solution)/shard_map/all_gather | solution.py:55
  89.1 9.6 %all-gather.6.cloned.1.call-done = bf16[1024,768]{1,0:T(8,128)(2,1)} async-done(((bf16[256,768]{1,0:T(8,128)(2,1)}), bf16[1024,768]{1,0:T(8,128)(2,1)}) %all-gather.6.cloned.1.call-update) | async-done | bytes 1572880 | tf_op jit(solution)/shard_map/all_gather | solution.py:75
  98.7 2.5 fusion.64
  102.9 1.7 exponential_reduce_fusion.1
  106.0 1.7 exponential_reduce_fusion
  107.8 1.9 convolution_convert_fusion.6
  109.7 1.9 convolution_convert_fusion.5
  112.3 1.8 convolution_convert_fusion.2
  114.8 33.6 %reduce-scatter.7.cloned.1.call-done = bf16[256,768]{1,0:T(8,128)(2,1)} async-done(((bf16[1024,768]{1,0:T(8,128)(2,1)}), bf16[256,768]{1,0:T(8,128)(2,1)}) %reduce-scatter.7.cloned.1.call-update) | async-done | bytes 393232 | tf_op jit(solution)/shard_map/reduce_scatter | solution.py:79
  150.9 2.0 add_convert_fusion.1
  153.6 1.7 collective-permute-start
  155.3 2.7 collective-permute-done
  158.9 8.7 %collective-permute-done.1 = bf16[768,192]{0,1:T(8,128)(2,1)S(1)} collective-permute-done((bf16[768,192]{0,1:T(8,128)(2,1)S(1)}, bf16[768,192]{0,1:T(8,128)(2,1)S(1)}, u32[]{:S(2)}, u32[]{:S(2)}) %collective-permute-start.1) | collective-permute-done | bytes 294944 | tf_op jit(solution)/shard_map/ppermute | solution.py:15
  169.9 14.8 %collective-permute-done.2 = bf16[768,384]{0,1:T(8,128)(2,1)} collective-permute-done((bf16[768,384]{0,1:T(8,128)(2,1)}, bf16[768,384]{0,1:T(8,128)(2,1)}, u32[]{:S(2)}, u32[]{:S(2)}) %collective-permute-start.2) | collective-permute-done | bytes 589856 | tf_op jit(solution)/shard_map/ppermute | solution.py:15
  184.7 6.4 %fusion.24 = bf16[768,768]{0,1:T(8,128)(2,1)} fusion(s32[]{:T(128)S(6)} %select_n.37, bf16[768,96]{0,1:T(8,128)(2,1)S(1)} %copy-done.6, bf16[768,96]{0,1:T(8,128)(2,1)S(1)} %collective-permute-done, bf16[768,192]{0,1:T(8,128)(2,1)} %copy-done.7, bf16[768,384]{0,1:T(8,128)(2,1)} %collective-permute-done.2), kind=kLoop, calls=%fused_computation.70 | loop fusion | flops 9437184 | bytes 2359300 | tf_op jit(solution)/shard_map/jit(_roll_dynamic)/concatenate | solution.py:19
  191.1 4.8 fusion.65
  195.9 30.3 %all-gather.12.cloned.1.call-done = bf16[1024,768]{1,0:T(8,128)(2,1)} async-done(((bf16[256,768]{1,0:T(8,128)(2,1)}), bf16[1024,768]{1,0:T(8,128)(2,1)}) %all-gather.12.cloned.1.call-update) | async-done | bytes 1572880 | tf_op jit(solution)/shard_map/all_gather | solution.py:85
  226.2 6.4 %convert_reduce_fusion = (f32[768]{0:T(1024)}, bf16[1024,768]{1,0:T(8,128)(2,1)S(1)}) fusion(f32[1024,768]{1,0:T(8,128)} %fusion.65, f32[768]{0:T(1024)S(1)} %dynamic-slice_convert_fusion, bf16[1024,768]{1,0:T(8,128)(2,1)} %all-gather.12.cloned.1.call-done, bf16[768,768]{0,1:T(8,128)(2,1)} %fusion.24), kind=kOutput, calls=%fused_computation.29 | convolution fusion | flops 1226046720 | bytes 7477248 | tf_op jit(solution)/shard_map/id,fd->if/dot_general | solution.py:231
  233.8 2.6 convolution_convert_fusion
  236.5 5.6 %convolution_convert_fusion.1 = bf16[1024,768]{1,0:T(8,128)(2,1)} fusion(bf16[768,768]{0,1:T(8,128)(2,1)} %fusion.24, f32[1024,768]{1,0:T(8,128)} %fusion.65, f32[768]{0:T(1024)S(1)} %dynamic-slice_convert_fusion), kind=kOutput, calls=%fused_computation.45 | convolution fusion | flops 1216610304 | bytes 5901312 | tf_op jit(solution)/shard_map/dot_general | solution.py:223
  242.1 28.6 %reduce-scatter.11.cloned.1.call-done = bf16[256,768]{1,0:T(8,128)(2,1)} async-done(((bf16[1024,768]{1,0:T(8,128)(2,1)}), bf16[256,768]{1,0:T(8,128)(2,1)}) %reduce-scatter.11.cloned.1.call-update) | async-done | bytes 393232 | tf_op jit(solution)/shard_map/reduce_scatter | solution.py:89
  270.7 2.1 fusion.48
  272.8 34.3 %reduce-scatter.9.cloned.1.call-done = bf16[256,768]{1,0:T(8,128)(2,1)} async-done(((bf16[1024,768]{1,0:T(8,128)(2,1)}), bf16[256,768]{1,0:T(8,128)(2,1)}) %reduce-scatter.9.cloned.1.call-update) | async-done | bytes 393232 | tf_op jit(solution)/shard_map/reduce_scatter | solution.py:79
  307.2 3.5 convert_reduce_fusion.6
  310.8 35.9 %all-gather.14.cloned.1.call-done = bf16[1024,768]{1,0:T(8,128)(2,1)} async-done(((bf16[256,768]{1,0:T(8,128)(2,1)}), bf16[1024,768]{1,0:T(8,128)(2,1)}) %all-gather.14.cloned.1.call-update) | async-done | bytes 1572880 | tf_op jit(solution)/shard_map/all_gather | solution.py:85
  346.7 2.2 convolution_convert_fusion.3
  349.0 4.7 fusion.57
  353.7 2.5 multiply_reduce_fusion.1
  356.2 2.2 multiply_convert_fusion.1
  360.3 2.5 multiply_reduce_fusion
  362.8 2.6 convert_reduce_fusion.8
  365.4 1.8 multiply_convert_fusion
  369.5 2.6 bitcast_convert_fusion
  372.2 5.1 %fusion.60 = f32[768,768]{0,1:T(8,128)} fusion(bf16[1024,768]{1,0:T(8,128)(2,1)S(1)} %copy-done.22, f32[1024,768]{1,0:T(8,128)} %fusion.65, f32[768]{0:T(1024)S(1)} %copy-done.20), kind=kOutput, calls=%fused_computation.138 | convolution fusion | flops 1215823872 | bytes 7080960 | tf_op jit(solution)/shard_map/if,id->fd/dot_general | solution.py:230
  377.6 4.8 fusion.67
  382.4 1.5 convolution_convert_fusion.4
  385.2 3.7 all-to-all-start.1
  389.0 2.5 fusion.68
  394.2 3.0 all-to-all-done.1
  397.2 3.6 all-to-all-start
  402.5 15.1 %all-to-all-done = bf16[8,96,3,192]{1,3,2,0:T(8,128)(2,1)S(1)} async-done(((bf16[8,96,3,192]{1,3,2,0:T(8,128)(2,1)}), bf16[8,96,3,192]{1,3,2,0:T(8,128)(2,1)S(1)}, u32[]{:S(2)}, u32[]{:S(2)}) %all-to-all-start) | async-done | bytes 884768 | tf_op jit(solution)/shard_map/all_to_all | solution.py:29
  418.7 1.5 fusion.49
  420.2 39.5 %all-reduce.16 = (f32[768]{0:T(1024)S(1)}, f32[768]{0:T(1024)S(1)}, f32[1536]{0:T(1024)S(1)}, f32[768]{0:T(1024)S(1)}, f32[768]{0:T(1024)S(1)}, /*index=5*/f32[7...) all-reduce(f32[768]{0:T(1024)S(1)} %get-tuple-element.31, ...), channel_id=6, replica_groups=mesh['dp'=8,'tensor'=4] {'dp','tensor'}, use_global_device_ids=true, to_apply=%region_19.21.clone | all-reduce | flops 9216 | bytes 73728
  464.4 2.2 fusion.42
  466.6 31.6 %reduce-scatter.15.cloned.1.call-done = f32[96,768]{1,0:T(8,128)} async-done(((f32[768,768]{1,0:T(8,128)}), f32[96,768]{1,0:T(8,128)}) %reduce-scatter.15.cloned.1.call-update) | async-done | bytes 294928 | tf_op jit(solution)/shard_map/reduce_scatter | solution.py:68
  (175 shorter events, 41.3 us)
Async XLA Ops:
  8.0 90.7 %all-gather.6.cloned.1.call-start = ((), (), s32[]{:S(2)}) async-start(), calls=%async_computation.8 | async-start | bytes 1966080 | tf_op jit(solution)/shard_map/all_gather | solution.py:75
  10.5 51.4 %copy-start.12 = (f32[256]{0:T(256)}, f32[256]{0:T(256)S(1)}, u32[]{:S(2)}) copy-start(f32[256]{0:T(256)S(1)} %add_rsqrt_fusion.1) | copy-start | bytes 3076
  59.6 28.2 %copy-start.24 = (s32[1,2]{1,0:T(1,128)S(1)}, s32[1,2]{1,0:T(1,128)}, u32[]{:S(2)}) copy-start(s32[1,2]{1,0:T(1,128)} %param.18) | copy-start | bytes 28
  61.6 86.8 %reduce-scatter.7.cloned.1.call-start = ((), (), s32[]{:S(2)}) async-start(), calls=%async_computation.9 | async-start | bytes 1966080 | tf_op jit(solution)/shard_map/reduce_scatter | solution.py:79
  77.5 23.7 %copy-start.8 = (bf16[768,3,192]{0,2,1:T(8,128)(2,1)}, bf16[768,3,192]{0,2,1:T(8,128)(2,1)S(1)}, u32[]{:S(2)}) copy-start(bf16[768,3,192]{0,2,1:T(8,128)(2,1)S(1)} %copy.33) | copy-start | bytes 2654212
  102.9 5.0 copy-start.1
  105.9 3.8 copy-start
  109.7 1.9 copy-start.10
  111.6 0.7 copy-start.11
  111.6 36.8 %copy-start.2 = (bf16[256,768]{1,0:T(8,128)(2,1)S(1)}, bf16[256,768]{1,0:T(8,128)(2,1)}, u32[]{:S(2)}) copy-start(bf16[256,768]{1,0:T(8,128)(2,1)} %param.17) | copy-start | bytes 1179652
  114.1 39.4 %copy-start.6 = (bf16[768,96]{0,1:T(8,128)(2,1)S(1)}, bf16[768,96]{0,1:T(8,128)(2,1)}, u32[]{:S(2)}) copy-start(bf16[768,96]{0,1:T(8,128)(2,1)} %param.29) | copy-start | bytes 442372
  114.2 76.9 %all-gather.10.cloned.1.call-start = ((), (), s32[]{:S(2)}) async-start(), calls=%async_computation.11 | async-start | bytes 1327104 | tf_op jit(solution)/shard_map/all_gather | solution.py:61
  114.7 76.3 %all-gather.8.cloned.1.call-start = ((), (), s32[]{:S(2)}) async-start(), calls=%async_computation.10 | async-start | bytes 1966080 | tf_op jit(solution)/shard_map/all_gather | solution.py:75
  152.9 73.3 %all-gather.12.cloned.1.call-start = ((), (), s32[]{:S(2)}) async-start(), calls=%async_computation.13 | async-start | bytes 1966080 | tf_op jit(solution)/shard_map/all_gather | solution.py:85
  153.5 117.2 %reduce-scatter.11.cloned.1.call-start = ((), (), s32[]{:S(2)}) async-start(), calls=%async_computation.14 | async-start | bytes 1966080 | tf_op jit(solution)/shard_map/reduce_scatter | solution.py:89
  153.6 4.4 collective-permute-start
  158.0 9.7 %collective-permute-start.1 = (bf16[768,192]{0,1:T(8,128)(2,1)S(1)}, bf16[768,192]{0,1:T(8,128)(2,1)S(1)}, u32[]{:S(2)}, u32[]{:S(2)}) collective-permute-start(bf16[768,192]{0,1:T(8,128)(2,1)S(1)} %pad_maximum_fusion.3), channel_id=1, source_target_pairs={{0,24},{4,28},{8,0},{12,4},{16,8},{20,12},{24,16},{28,20},{1,25},{... | collective-permute-start | bytes 884744 | tf_op jit(solution)/shard_map/ppermute | solution.py:15
  167.7 0.7 copy-start.7
  169.2 15.4 %collective-permute-start.2 = (bf16[768,384]{0,1:T(8,128)(2,1)}, bf16[768,384]{0,1:T(8,128)(2,1)}, u32[]{:S(2)}, u32[]{:S(2)}) collective-permute-start(bf16[768,384]{0,1:T(8,128)(2,1)} %pad_maximum_fusion.1), channel_id=1, source_target_pairs={{0,16},{4,20},{8,24},{12,28},{16,0},{20,4},{24,8},{28,12},{1,17},{... | collective-permute-start | bytes 1769480 | tf_op jit(solution)/shard_map/ppermute | solution.py:15
  169.9 66.6 %copy-start.19 = (f32[768]{0:T(1024)}, f32[768]{0:T(1024)S(1)}, u32[]{:S(2)}) copy-start(f32[768]{0:T(1024)S(1)} %dynamic-slice_convert_fusion) | copy-start | bytes 9220
  226.2 7.6 %copy-start.23 = (bf16[768,768]{1,0:T(8,128)(2,1)S(1)}, bf16[768,768]{1,0:T(8,128)(2,1)}, u32[]{:S(2)}) copy-start(bf16[768,768]{1,0:T(8,128)(2,1)} %all-gather.10.cloned.1.call-done) | copy-start | bytes 3538948
  232.6 1.2 copy-start.25
  236.4 34.3 %copy-start.3 = (bf16[256,768]{1,0:T(8,128)(2,1)S(1)}, bf16[256,768]{1,0:T(8,128)(2,1)}, u32[]{:S(2)}) copy-start(bf16[256,768]{1,0:T(8,128)(2,1)} %reduce-scatter.7.cloned.1.call-done) | copy-start | bytes 1179652
  236.4 70.8 %reduce-scatter.9.cloned.1.call-start = ((), (), s32[]{:S(2)}) async-start(), calls=%async_computation.12 | async-start | bytes 1966080 | tf_op jit(solution)/shard_map/reduce_scatter | solution.py:79
  242.0 104.7 %all-gather.14.cloned.1.call-start = ((), (), s32[]{:S(2)}) async-start(), calls=%async_computation.15 | async-start | bytes 1966080 | tf_op jit(solution)/shard_map/all_gather | solution.py:85
  310.7 108.0 %reduce-scatter.13.cloned.1.call-start = ((), (), s32[]{:S(2)}) async-start(), calls=%async_computation.16 | async-start | bytes 1966080 | tf_op jit(solution)/shard_map/reduce_scatter | solution.py:89
  346.7 7.0 %slice-start.2 = ((s8[6291456]{0:T(1024)(128)(4,1)}), s8[4194304]{0:T(1024)(128)(4,1)S(1)}, s32[]{:S(2)}) async-start(s8[6291456]{0:T(1024)(128)(4,1)} %bitcast.96), calls=%async_computation.21 | async-start | bytes 8388608
  349.0 4.7 slice-start.3
  353.7 6.5 %slice-start = ((s8[6291456]{0:T(1024)(128)(4,1)}), s8[4194304]{0:T(1024)(128)(4,1)S(1)}, s32[]{:S(2)}) async-start(s8[6291456]{0:T(1024)(128)(4,1)} %bitcast.94), calls=%async_computation.19 | async-start | bytes 8388608
  356.2 4.1 slice-start.1
  368.3 1.2 copy-start.9
  369.5 2.7 copy-start.20
  369.5 2.7 copy-start.22
  372.1 94.5 %reduce-scatter.17.cloned.1.call-start = ((), (), s32[]{:S(2)}) async-start(), calls=%async_computation.18 | async-start | bytes 2654208 | tf_op jit(solution)/shard_map/reduce_scatter | solution.py:69
  377.3 5.1 %copy-start.5 = (bf16[1024,768]{1,0:T(8,128)(2,1)S(1)}, bf16[1024,768]{1,0:T(8,128)(2,1)}, u32[]{:S(2)}) copy-start(bf16[1024,768]{1,0:T(8,128)(2,1)} %all-gather.14.cloned.1.call-done) | copy-start | bytes 4718596
  377.3 120.8 %reduce-scatter.15.cloned.1.call-start = ((), (), s32[]{:S(2)}) async-start(), calls=%async_computation.17 | async-start | bytes 2654208 | tf_op jit(solution)/shard_map/reduce_scatter | solution.py:68
  385.2 12.0 %all-to-all-start.1 = ((bf16[8,192,96]{2,1,0:T(8,128)(2,1)}), bf16[8,192,96]{2,1,0:T(8,128)(2,1)S(1)}, u32[]{:S(2)}, u32[]{:S(2)}) async-start(bf16[8,192,96]{2,1,0:T(8,128)(2,1)} %bitcast.92), calls=%async_computation.5 | async-start | bytes 786432 | tf_op jit(solution)/shard_map/all_to_all | solution.py:29
  391.6 9.2 %copy-start.18 = (f32[768]{0:T(1024)S(1)}, f32[768]{0:T(1024)}, u32[]{:S(2)}) copy-start(f32[768]{0:T(1024)} %get-tuple-element.78) | copy-start | bytes 9220
  391.7 9.5 %copy-start.21 = (f32[3,64]{1,0:T(4,128)S(1)}, f32[3,64]{1,0:T(4,128)}, u32[]{:S(2)}) copy-start(f32[3,64]{1,0:T(4,128)} %get-tuple-element.76) | copy-start | bytes 2308
  392.9 25.8 %copy-start.13 = (f32[256]{0:T(256)S(1)}, f32[256]{0:T(256)}, u32[]{:S(2)}) copy-start(f32[256]{0:T(256)} %copy-done.12) | copy-start | bytes 3076
  394.2 26.0 %copy-start.14 = (f32[768]{0:T(1024)S(1)}, f32[768]{0:T(1024)}, u32[]{:S(2)}) copy-start(f32[768]{0:T(1024)} %get-tuple-element.29) | copy-start | bytes 9220
  394.2 26.0 %copy-start.15 = (f32[768]{0:T(1024)S(1)}, f32[768]{0:T(1024)}, u32[]{:S(2)}) copy-start(f32[768]{0:T(1024)} %get-tuple-element.35) | copy-start | bytes 9220
  394.2 26.0 %copy-start.16 = (f32[768]{0:T(1024)S(1)}, f32[768]{0:T(1024)}, u32[]{:S(2)}) copy-start(f32[768]{0:T(1024)} %get-tuple-element.53) | copy-start | bytes 9220
  394.2 26.0 %copy-start.17 = (f32[768]{0:T(1024)S(1)}, f32[768]{0:T(1024)}, u32[]{:S(2)}) copy-start(f32[768]{0:T(1024)} %get-tuple-element.59) | copy-start | bytes 9220
  394.2 70.2 %copy-start.4 = (f32[256,768]{1,0:T(8,128)S(1)}, f32[256,768]{1,0:T(8,128)}, u32[]{:S(2)}) copy-start(f32[256,768]{1,0:T(8,128)} %get-tuple-element.55) | copy-start | bytes 2359300
  397.2 20.3 %all-to-all-start = ((bf16[8,96,3,192]{1,3,2,0:T(8,128)(2,1)}), bf16[8,96,3,192]{1,3,2,0:T(8,128)(2,1)S(1)}, u32[]{:S(2)}, u32[]{:S(2)}) async-start(bf16[8,96,3,192]{1,3,2,0:T(8,128)(2,1)} %copy.37), calls=%async_computation.4 | async-start | bytes 2359296 | tf_op jit(solution)/shard_map/all_to_all | solution.py:29
Sparse Core Ops, SparseCore 0:
  61.7 36.9 all-gather.5
  114.3 34.1 reduce-scatter.6
  236.5 34.1 reduce-scatter.10
  272.9 34.2 reduce-scatter.8
Sparse Core Ops, SparseCore 1:
  116.5 22.7 all-gather.9
  153.0 35.9 all-gather.7
  190.4 35.8 all-gather.11
  310.8 35.9 all-gather.13
  372.2 34.1 reduce-scatter.12
  410.3 41.3 reduce-scatter.16
  455.8 42.3 reduce-scatter.14
